TPU v7x, 128 devices: a whole 4x4x4 slice. The times are simulated.
128 devices in a mesh: seq: 32 (over y, x, core), vis: 4 (over z).
Axes of the slice: x: 4, y: 4, z: 4, core: 2. Of those that a mesh axis runs over, the one named last changes fastest.
Arguments:
- queries: bfloat16 [65536, 4096], P('seq', 'vis'), may hold values from -8 to 8
- latent_keys: bfloat16 [256, 64, 4096], P('seq', 'vis'), may hold values from -6 to 6
- latent_values: bfloat16 [256, 64, 4096], P('seq', 'vis'), may hold values from -6 to 6
- gate_vector: float32 [4096], P('vis'), may hold values from -1.2 to 1.2
- cotangent: bfloat16 [65536, 4096], P('seq', 'vis'), may hold values from -48 to 48
- image_slot: int32 [256], replicated, may hold values from 0 to 255, as said below
- image_lists: int32 [128, 12], replicated, may hold values from 0 to 255, as said below
Outputs:
- gated_output: bfloat16 [65536, 4096], P('seq', 'vis')
- grad_queries: bfloat16 [65536, 4096], P('seq', 'vis')
- grad_keys: bfloat16 [256, 64, 4096], P('seq', 'vis')
- grad_values: bfloat16 [256, 64, 4096], P('seq', 'vis')
- grad_gate: float32 [4096], P('vis')
Inputs may be any that keep to these rules, and one draw needn't show every extreme that they name: A permutation: image i, of document i // 32, is stored at slot image_slot[i], that is on index image_slot[i] // 8 of seq; every index of seq stores exactly one image of each of the 8 documents and no others. `image_lists`: row b names 12 distinct images, all of the document of block b, that is ids d * 32 to (d + 1) * 32 - 1 with d = b * 512 // 8192; the 4 blocks of each aligned run of 2048 tokens together name every one of the 32 images of their document (possible since 12 * 4 >= 32).
All inputs are finite; a program needn't handle non-finite values.
Results may differ from a plain program's by a relative error of at most 0.0099.
Values may be sent and summed in bfloat16 or wider, within the bound.
A program may use at most 256 MiB of HBM per device.

v0:
```python
import math

import jax
import jax.numpy as jnp
from jax import lax
from jax.sharding import PartitionSpec as P

HD = 128
LAT = 64
IMG_DOC = 32
DOC_TOK = 8192
BLK = 512
ATT = 12


def contract_last(left, right):
    return lax.dot_general(
        left, right, (((1,), (1,)), ((), ())), preferred_element_type=jnp.float32
    )


def contract_first(left, right):
    return lax.dot_general(
        left, right, (((0,), (0,)), ((), ())), preferred_element_type=jnp.float32
    )


def local(queries, latent_keys, latent_values, gate_vector, cotangent, image_slot, image_lists):
    seq_count = lax.axis_size("seq")
    seq_index = lax.axis_index("seq")
    tok_rows, head_cols = queries.shape
    own_images = latent_keys.shape[0]
    heads_here = head_cols // HD
    images_all = image_slot.shape[0]
    docs_all = images_all // IMG_DOC
    per_peer = max(1, own_images // docs_all)
    receive_rows = seq_count * per_peer
    blocks_here = tok_rows // BLK
    score_scale = 1.0 / math.sqrt(HD)
    flat_cols = LAT * head_cols
    slot_range = jnp.arange(images_all, dtype=jnp.int32)
    image_of_slot = jnp.sum(
        jnp.where(image_slot[None, :] == slot_range[:, None], slot_range[None, :], 0), axis=1
    )
    local_images = lax.dynamic_slice_in_dim(image_of_slot, seq_index * own_images, own_images, 0)
    local_docs = local_images // IMG_DOC
    peer_docs = jnp.arange(seq_count, dtype=jnp.int32) * tok_rows // DOC_TOK
    matches = local_docs[None, :] == peer_docs[:, None]
    doc_ranks = jnp.cumsum(matches.astype(jnp.int32), axis=1) - 1
    member = jnp.arange(per_peer, dtype=jnp.int32)
    picked = matches[:, None, :] & (doc_ranks[:, None, :] == member[None, :, None])
    own_range = jnp.arange(own_images, dtype=jnp.int32)
    send_index = jnp.sum(jnp.where(picked, own_range[None, None, :], 0), axis=2).reshape(
        receive_rows
    )
    send_valid = jnp.any(picked, axis=2).reshape(receive_rows)
    my_doc = seq_index * tok_rows // DOC_TOK
    doc_images = my_doc * IMG_DOC + jnp.arange(IMG_DOC, dtype=jnp.int32)
    doc_slots = image_slot[doc_images]
    doc_owner = doc_slots // own_images
    earlier = (doc_owner[None, :] == doc_owner[:, None]) & (doc_slots[None, :] < doc_slots[:, None])
    receive_pos = doc_owner * per_peer + jnp.sum(earlier.astype(jnp.int32), axis=1)
    fetched_keys, fetched_values = (
        lax.all_to_all(
            lax.all_to_all(latent_keys[send_index], "seq", split_axis=0, concat_axis=0, tiled=True),
            "vis",
            split_axis=2,
            concat_axis=1,
            tiled=True,
        ),
        lax.all_to_all(
            lax.all_to_all(
                latent_values[send_index], "seq", split_axis=0, concat_axis=0, tiled=True
            ),
            "vis",
            split_axis=2,
            concat_axis=1,
            tiled=True,
        ),
    )
    block_lists = lax.dynamic_slice_in_dim(image_lists, seq_index * blocks_here, blocks_here, 0)
    block_pos = receive_pos[block_lists - my_doc * IMG_DOC]
    tanh_gate = jnp.tanh(gate_vector)
    tanh_slope = 1.0 - tanh_gate * tanh_gate
    row_range = jnp.arange(receive_rows, dtype=jnp.int32)
    key_sum = jnp.zeros((receive_rows, flat_cols), jnp.float32)
    value_sum = jnp.zeros((receive_rows, flat_cols), jnp.float32)
    gate_part = jnp.zeros((head_cols,), jnp.float32)
    gated_parts = []
    query_parts = []
    for block_id in range(blocks_here):
        row_start = block_id * BLK
        query_block = queries[row_start : row_start + BLK]
        cot_block = cotangent[row_start : row_start + BLK].astype(jnp.float32)
        grad_attn = (cot_block * tanh_gate).astype(jnp.bfloat16)
        positions = block_pos[block_id]
        key_block = fetched_keys[positions].reshape(ATT * LAT, head_cols)
        value_block = fetched_values[positions].reshape(ATT * LAT, head_cols)
        attended_cols = []
        query_cols = []
        key_cols = []
        value_cols = []
        for head in range(heads_here):
            low = head * HD
            high = low + HD
            query_head = query_block[:, low:high]
            key_head = key_block[:, low:high]
            value_head = value_block[:, low:high]
            grad_head = grad_attn[:, low:high]
            scores = contract_last(query_head, key_head) * score_scale
            row_max = jnp.max(scores, axis=1, keepdims=True)
            raised = jnp.exp(scores - row_max)
            weights = raised / jnp.sum(raised, axis=1, keepdims=True)
            weights_low = weights.astype(jnp.bfloat16)
            attended = jnp.dot(weights_low, value_head, preferred_element_type=jnp.float32)
            attended_cols.append(attended)
            row_dot = jnp.sum(grad_head.astype(jnp.float32) * attended, axis=1, keepdims=True)
            grad_weights = contract_last(grad_head, value_head)
            grad_scores = (weights * (grad_weights - row_dot) * score_scale).astype(jnp.bfloat16)
            query_cols.append(jnp.dot(grad_scores, key_head, preferred_element_type=jnp.float32))
            key_cols.append(contract_first(grad_scores, query_head))
            value_cols.append(contract_first(weights_low, grad_head))
        attended_flat = jnp.concatenate(attended_cols, 1)
        gated_parts.append((tanh_gate * attended_flat).astype(jnp.bfloat16))
        gate_part = gate_part + jnp.sum(cot_block * attended_flat * tanh_slope, axis=0)
        query_parts.append(jnp.concatenate(query_cols, 1).astype(jnp.bfloat16))
        key_term = jnp.concatenate(key_cols, 1).reshape(ATT, flat_cols)
        value_term = jnp.concatenate(value_cols, 1).reshape(ATT, flat_cols)
        placing = (row_range[:, None] == positions[None, :]).astype(jnp.float32)
        key_sum = key_sum + jnp.dot(placing, key_term, precision=lax.Precision.HIGHEST)
        value_sum = value_sum + jnp.dot(placing, value_term, precision=lax.Precision.HIGHEST)
    grad_gate = lax.psum(gate_part, "seq")
    part_keys = key_sum.reshape(receive_rows, LAT, head_cols).astype(jnp.bfloat16)
    part_values = value_sum.reshape(receive_rows, LAT, head_cols).astype(jnp.bfloat16)
    fold_table = ((send_index[None, :] == own_range[:, None]) & send_valid[None, :]).astype(
        jnp.bfloat16
    )
    back_keys, back_values = (
        lax.all_to_all(
            lax.all_to_all(part_keys, "seq", split_axis=0, concat_axis=0, tiled=True),
            "vis",
            split_axis=1,
            concat_axis=2,
            tiled=True,
        ),
        lax.all_to_all(
            lax.all_to_all(part_values, "seq", split_axis=0, concat_axis=0, tiled=True),
            "vis",
            split_axis=1,
            concat_axis=2,
            tiled=True,
        ),
    )
    grad_keys = jnp.einsum(
        "or,rlc->olc", fold_table, back_keys, preferred_element_type=jnp.float32
    ).astype(jnp.bfloat16)
    grad_values = jnp.einsum(
        "or,rlc->olc", fold_table, back_values, preferred_element_type=jnp.float32
    ).astype(jnp.bfloat16)
    gated_output = jnp.concatenate(gated_parts, 0)
    grad_queries = jnp.concatenate(query_parts, 0)
    return (gated_output, grad_queries, grad_keys, grad_values, grad_gate)


def solution(mesh):
    in_specs = (
        P("seq", "vis"),
        P("seq", "vis", None),
        P("seq", "vis", None),
        P("vis"),
        P("seq", "vis"),
        P(),
        P(),
    )
    out_specs = (
        P("seq", "vis"),
        P("seq", "vis"),
        P("seq", "vis", None),
        P("seq", "vis", None),
        P("vis"),
    )
    return jax.shard_map(local, mesh=mesh, in_specs=in_specs, out_specs=out_specs, check_vma=False)
```

profile of v0, /device:TPU:1, one launch (start us, length us, event | category | flops | bytes accessed | tf_op | source)
XLA Modules:
  0.0 963.9 jit_solution(17850808473397298905)
XLA Ops:
  5.7 8.8 all-to-all-start
  17.4 47.4 %all-to-all-done = bf16[32,16,4096]{2,1,0:T(8,128)(2,1)} async-done(((bf16[32,16,4096]{2,1,0:T(8,128)(2,1)}), bf16[32,16,4096]{2,1,0:T(8,128)(2,1)}, u32[]{:S(2)}, u32[]{:S(2)}) %all-to-all-start) | async-done | bytes 4194336 | tf_op jit(solution)/shard_map/all_to_all | solution.py:65
  64.8 8.0 all-to-all-start.2
  72.8 23.7 %copy.334 = bf16[32,16,4096]{0,1,2:T(8,128)(2,1)} copy(bf16[32,16,4096]{2,1,0:T(8,128)(2,1)} %all-to-all-done) | data formatting | bytes 8388608 | tf_op jit(solution)/shard_map/all_to_all | solution.py:65
  96.5 19.2 %reshape.597 = bf16[4,2,262144]{2,1,0:T(2,128)(2,1)} reshape(bf16[4096,16,32]{2,1,0:T(8,128)(2,1)} %bitcast.427) | data formatting | bytes 8388608
  115.7 7.4 all-to-all-done.2
  123.1 5.5 all-to-all-start.1
  129.7 3.8 fusion.490
  141.5 23.7 %copy.338 = bf16[32,16,4096]{0,1,2:T(8,128)(2,1)} copy(bf16[32,16,4096]{2,1,0:T(8,128)(2,1)} %all-to-all-done.2) | data formatting | bytes 8388608 | tf_op jit(solution)/shard_map/all_to_all | solution.py:72
  165.3 19.2 %reshape.599 = bf16[4,2,262144]{2,1,0:T(2,128)(2,1)} reshape(bf16[4096,16,32]{2,1,0:T(8,128)(2,1)} %bitcast.428) | data formatting | bytes 8388608
  184.4 4.9 all-to-all-start.3
  189.4 12.0 %reshape.598 = bf16[4096,16,32]{2,1,0:T(8,128)(2,1)} reshape(bf16[4,2,262144]{2,1,0:T(2,128)(2,1)} %all-to-all-done.1) | data formatting | bytes 8388608
  201.4 20.2 %copy.425 = bf16[32,16,4,1024]{3,2,1,0:T(4,128)(2,1)} copy(bf16[32,16,4,1024]{0,1,3,2:T(8,128)(2,1)} %bitcast.429) | data formatting | bytes 8388608 | tf_op jit(solution)/shard_map/all_to_all | solution.py:64
  221.6 5.9 copy.336
  285.2 4.1 gather_fusion.10
  319.0 12.0 %reshape.600 = bf16[4096,16,32]{2,1,0:T(8,128)(2,1)} reshape(bf16[4,2,262144]{2,1,0:T(2,128)(2,1)} %all-to-all-done.3) | data formatting | bytes 8388608
  331.1 20.1 %copy.426 = bf16[32,16,4,1024]{3,2,1,0:T(4,128)(2,1)} copy(bf16[32,16,4,1024]{0,1,3,2:T(8,128)(2,1)} %bitcast.430) | data formatting | bytes 8388608 | tf_op jit(solution)/shard_map/all_to_all | solution.py:71
  351.1 6.0 copy.340
  357.1 4.0 gather_fusion.11
  361.1 4.0 gather_fusion.9
  365.2 4.0 gather_fusion.7
  369.2 4.2 gather_fusion.5
  441.4 8.5 fusion.7
  545.4 3.5 copy.378
  548.9 4.1 reshape.479
  569.9 3.5 copy.379
  573.5 4.1 reshape.480
  594.4 3.5 copy.380
  598.0 4.1 reshape.481
  618.9 3.5 copy.377
  622.5 4.0 reshape.478
  626.5 5.6 fusion.463
  632.1 4.1 convolution_add_fusion.5
  636.3 4.1 convolution_add_fusion.4
  640.4 4.1 fusion
  644.5 4.3 copy.431
  648.9 8.6 all-to-all-start.4
  658.7 3.5 copy.383
  662.3 4.0 reshape.482
  666.2 3.6 copy.386
  669.8 4.0 reshape.485
  673.8 3.5 copy.385
  677.3 4.1 reshape.484
  686.8 3.5 copy.384
  690.4 3.9 reshape.483
  694.3 5.9 fusion.462
  700.2 4.1 convolution_add_fusion.2
  704.3 4.1 convolution_add_fusion.1
  708.4 4.1 fusion.1
  712.5 4.3 copy.432
  716.9 7.8 all-to-all-start.6
  738.4 6.5 copy.381
  744.9 30.1 %all-to-all-done.6 = bf16[32,64,1024]{2,1,0:T(8,128)(2,1)} async-done(((bf16[32,64,1024]{2,1,0:T(8,128)(2,1)}), bf16[32,64,1024]{2,1,0:T(8,128)(2,1)}, u32[]{:S(2)}, u32[]{:S(2)}) %all-to-all-start.6) | async-done | bytes 4194336 | tf_op jit(solution)/shard_map/all_to_all | solution.py:147
  775.0 4.9 all-to-all-start.5
  796.2 6.5 copy.387
  802.7 23.1 %all-to-all-done.5 = bf16[32,64,1024]{2,0,1:T(8,128)(2,1)} async-done(((bf16[32,64,1024]{2,0,1:T(8,128)(2,1)}), bf16[32,64,1024]{2,0,1:T(8,128)(2,1)}, u32[]{:S(2)}, u32[]{:S(2)}) %all-to-all-start.5) | async-done | bytes 4194336 | tf_op jit(solution)/shard_map/all_to_all | solution.py:139
  825.8 4.9 all-to-all-start.7
  840.5 6.6 copy.390
  850.3 6.4 copy.389
  856.8 67.0 %psum.7 = f32[1024]{0:T(1024)} all-reduce(f32[1024]{0:T(1024)S(1)} %add_add_fusion), channel_id=1, replica_groups=mesh['seq'=32,'vis'=4] {'seq'}, use_global_device_ids=true, to_apply=%region_105.106 | all-reduce | flops 1024 | bytes 8192 | tf_op jit(solution)/shard_map/psum | solution.py:132
  923.7 7.7 copy.436
  931.4 7.8 all_to_all.78
  943.6 7.7 copy.435
  951.3 7.8 all_to_all.83
  (787 shorter events, 376.2 us)
Async XLA Ops:
  5.7 8.8 copy-start.5
  5.7 59.0 %all-to-all-start = ((bf16[32,16,4096]{2,1,0:T(8,128)(2,1)}), bf16[32,16,4096]{2,1,0:T(8,128)(2,1)}, u32[]{:S(2)}, u32[]{:S(2)}) async-start(bf16[32,16,4096]{2,1,0:T(8,128)(2,1)} %gather_fusion), calls=%async_computation | async-start | bytes 8388608 | tf_op jit(solution)/shard_map/all_to_all | solution.py:65
  64.8 58.4 %all-to-all-start.2 = ((bf16[32,16,4096]{2,1,0:T(8,128)(2,1)}), bf16[32,16,4096]{2,1,0:T(8,128)(2,1)}, u32[]{:S(2)}, u32[]{:S(2)}) async-start(bf16[32,16,4096]{2,1,0:T(8,128)(2,1)} %gather_fusion.4), calls=%async_computation.2 | async-start | bytes 8388608 | tf_op jit(solution)/shard_map/all_to_all | solution.py:72
  115.7 13.0 %copy-start.2 = (s32[256]{0:T(256)S(1)}, s32[256]{0:T(256)}, u32[]{:S(2)}) copy-start(s32[256]{0:T(256)} %param.12) | copy-start | bytes 3076
  115.7 13.7 %copy-start.183 = (s32[128,12]{0,1:T(8,128)S(1)}, s32[128,12]{0,1:T(8,128)}, u32[]{:S(2)}) copy-start(s32[128,12]{0,1:T(8,128)} %param.13) | copy-start | bytes 18436
  123.1 61.3 %all-to-all-start.1 = ((bf16[4,2,262144]{2,1,0:T(2,128)(2,1)}), bf16[4,2,262144]{2,1,0:T(2,128)(2,1)}, u32[]{:S(2)}, u32[]{:S(2)}) async-start(bf16[4,2,262144]{2,1,0:T(2,128)(2,1)} %reshape.597), calls=%async_computation.1 | async-start | bytes 8388608 | tf_op jit(solution)/shard_map/all_to_all | solution.py:64
  184.4 134.6 %all-to-all-start.3 = ((bf16[4,2,262144]{2,1,0:T(2,128)(2,1)}), bf16[4,2,262144]{2,1,0:T(2,128)(2,1)}, u32[]{:S(2)}, u32[]{:S(2)}) async-start(bf16[4,2,262144]{2,1,0:T(2,128)(2,1)} %reshape.599), calls=%async_computation.3 | async-start | bytes 8388608 | tf_op jit(solution)/shard_map/all_to_all | solution.py:71
  230.4 17.2 %copy-start.10 = (bf16[12,64,1024]{2,1,0:T(8,128)(2,1)}, bf16[12,64,1024]{2,1,0:T(8,128)(2,1)S(1)}, u32[]{:S(2)}) copy-start(bf16[12,64,1024]{2,1,0:T(8,128)(2,1)S(1)} %gather_fusion.6) | copy-start | bytes 4718596
  233.0 219.3 %copy-start.173 = (f32[512]{0:T(512)}, f32[512]{0:T(512)S(1)}, u32[]{:S(2)}) copy-start(f32[512]{0:T(512)S(1)} %get-tuple-element.128) | copy-start | bytes 6148
  235.4 226.9 %copy-start.175 = (f32[512]{0:T(512)}, f32[512]{0:T(512)S(1)}, u32[]{:S(2)}) copy-start(f32[512]{0:T(512)S(1)} %get-tuple-element.124) | copy-start | bytes 6148
  237.8 224.0 %copy-start.177 = (f32[512]{0:T(512)}, f32[512]{0:T(512)S(1)}, u32[]{:S(2)}) copy-start(f32[512]{0:T(512)S(1)} %get-tuple-element.120) | copy-start | bytes 6148
  240.2 220.1 %copy-start.179 = (f32[512]{0:T(512)}, f32[512]{0:T(512)S(1)}, u32[]{:S(2)}) copy-start(f32[512]{0:T(512)S(1)} %get-tuple-element.116) | copy-start | bytes 6148
  242.7 216.2 %copy-start.181 = (f32[512]{0:T(512)}, f32[512]{0:T(512)S(1)}, u32[]{:S(2)}) copy-start(f32[512]{0:T(512)S(1)} %get-tuple-element.112) | copy-start | bytes 6148
  252.8 17.3 %copy-start.14 = (bf16[12,64,1024]{2,1,0:T(8,128)(2,1)}, bf16[12,64,1024]{2,1,0:T(8,128)(2,1)S(1)}, u32[]{:S(2)}) copy-start(bf16[12,64,1024]{2,1,0:T(8,128)(2,1)S(1)} %gather_fusion.3) | copy-start | bytes 4718596
  275.3 21.4 %copy-start.12 = (bf16[12,64,1024]{2,1,0:T(8,128)(2,1)}, bf16[12,64,1024]{2,1,0:T(8,128)(2,1)S(1)}, u32[]{:S(2)}) copy-start(bf16[12,64,1024]{2,1,0:T(8,128)(2,1)S(1)} %gather_fusion.8) | copy-start | bytes 4718596
  373.6 78.6 %copy-start.190 = (f32[512]{0:T(512)}, f32[512]{0:T(512)S(1)}, u32[]{:S(2)}) copy-start(f32[512]{0:T(512)S(1)} %fusion.109) | copy-start | bytes 6148
  375.1 87.3 %copy-start.192 = (f32[512]{0:T(512)}, f32[512]{0:T(512)S(1)}, u32[]{:S(2)}) copy-start(f32[512]{0:T(512)S(1)} %fusion.107) | copy-start | bytes 6148
  375.5 86.3 %copy-start.194 = (f32[512]{0:T(512)}, f32[512]{0:T(512)S(1)}, u32[]{:S(2)}) copy-start(f32[512]{0:T(512)S(1)} %fusion.105) | copy-start | bytes 6148
  376.6 83.8 %copy-start.196 = (f32[512]{0:T(512)}, f32[512]{0:T(512)S(1)}, u32[]{:S(2)}) copy-start(f32[512]{0:T(512)S(1)} %fusion.103) | copy-start | bytes 6148
  377.0 26.4 %copy-start.198 = (f32[512]{0:T(512)}, f32[512]{0:T(512)S(1)}, u32[]{:S(2)}) copy-start(f32[512]{0:T(512)S(1)} %fusion.101) | copy-start | bytes 6148
  378.1 24.2 %copy-start.201 = (f32[512]{0:T(512)}, f32[512]{0:T(512)S(1)}, u32[]{:S(2)}) copy-start(f32[512]{0:T(512)S(1)} %fusion.99) | copy-start | bytes 6148
  378.6 21.4 %copy-start.203 = (f32[512]{0:T(512)}, f32[512]{0:T(512)S(1)}, u32[]{:S(2)}) copy-start(f32[512]{0:T(512)S(1)} %fusion.97) | copy-start | bytes 6148
  379.6 18.3 %copy-start.253 = (f32[512]{0:T(512)}, f32[512]{0:T(512)S(1)}, u32[]{:S(2)}) copy-start(f32[512]{0:T(512)S(1)} %fusion.95) | copy-start | bytes 6148
  380.1 39.3 %copy-start.221 = (f32[512]{0:T(512)}, f32[512]{0:T(512)S(1)}, u32[]{:S(2)}) copy-start(f32[512]{0:T(512)S(1)} %fusion.93) | copy-start | bytes 6148
  381.1 36.9 %copy-start.225 = (f32[512]{0:T(512)}, f32[512]{0:T(512)S(1)}, u32[]{:S(2)}) copy-start(f32[512]{0:T(512)S(1)} %fusion.91) | copy-start | bytes 6148
  381.6 35.2 %copy-start.229 = (f32[512]{0:T(512)}, f32[512]{0:T(512)S(1)}, u32[]{:S(2)}) copy-start(f32[512]{0:T(512)S(1)} %fusion.89) | copy-start | bytes 6148
  382.7 32.9 %copy-start.233 = (f32[512]{0:T(512)}, f32[512]{0:T(512)S(1)}, u32[]{:S(2)}) copy-start(f32[512]{0:T(512)S(1)} %fusion.87) | copy-start | bytes 6148
  383.1 31.2 %copy-start.237 = (f32[512]{0:T(512)}, f32[512]{0:T(512)S(1)}, u32[]{:S(2)}) copy-start(f32[512]{0:T(512)S(1)} %fusion.85) | copy-start | bytes 6148
  384.2 28.9 %copy-start.241 = (f32[512]{0:T(512)}, f32[512]{0:T(512)S(1)}, u32[]{:S(2)}) copy-start(f32[512]{0:T(512)S(1)} %fusion.83) | copy-start | bytes 6148
  384.6 27.2 %copy-start.245 = (f32[512]{0:T(512)}, f32[512]{0:T(512)S(1)}, u32[]{:S(2)}) copy-start(f32[512]{0:T(512)S(1)} %fusion.81) | copy-start | bytes 6148
  385.7 24.9 %copy-start.247 = (f32[512]{0:T(512)}, f32[512]{0:T(512)S(1)}, u32[]{:S(2)}) copy-start(f32[512]{0:T(512)S(1)} %fusion.79) | copy-start | bytes 6148
  386.2 43.2 %copy-start.205 = (f32[512]{0:T(512)}, f32[512]{0:T(512)S(1)}, u32[]{:S(2)}) copy-start(f32[512]{0:T(512)S(1)} %fusion.125) | copy-start | bytes 6148
  387.2 40.9 %copy-start.207 = (f32[512]{0:T(512)}, f32[512]{0:T(512)S(1)}, u32[]{:S(2)}) copy-start(f32[512]{0:T(512)S(1)} %fusion.123) | copy-start | bytes 6148
  387.7 39.2 %copy-start.209 = (f32[512]{0:T(512)}, f32[512]{0:T(512)S(1)}, u32[]{:S(2)}) copy-start(f32[512]{0:T(512)S(1)} %fusion.121) | copy-start | bytes 6148
  388.8 36.9 %copy-start.211 = (f32[512]{0:T(512)}, f32[512]{0:T(512)S(1)}, u32[]{:S(2)}) copy-start(f32[512]{0:T(512)S(1)} %fusion.119) | copy-start | bytes 6148
  389.2 35.2 %copy-start.213 = (f32[512]{0:T(512)}, f32[512]{0:T(512)S(1)}, u32[]{:S(2)}) copy-start(f32[512]{0:T(512)S(1)} %fusion.117) | copy-start | bytes 6148
  390.3 32.9 %copy-start.215 = (f32[512]{0:T(512)}, f32[512]{0:T(512)S(1)}, u32[]{:S(2)}) copy-start(f32[512]{0:T(512)S(1)} %fusion.115) | copy-start | bytes 6148
  390.7 31.3 %copy-start.217 = (f32[512]{0:T(512)}, f32[512]{0:T(512)S(1)}, u32[]{:S(2)}) copy-start(f32[512]{0:T(512)S(1)} %fusion.113) | copy-start | bytes 6148
  391.8 28.8 %copy-start.251 = (f32[512]{0:T(512)}, f32[512]{0:T(512)S(1)}, u32[]{:S(2)}) copy-start(f32[512]{0:T(512)S(1)} %fusion.111) | copy-start | bytes 6148
  392.3 46.6 %copy-start.219 = (f32[512]{0:T(512)}, f32[512]{0:T(512)S(1)}, u32[]{:S(2)}) copy-start(f32[512]{0:T(512)S(1)} %fusion.141) | copy-start | bytes 6148
  393.3 44.4 %copy-start.223 = (f32[512]{0:T(512)}, f32[512]{0:T(512)S(1)}, u32[]{:S(2)}) copy-start(f32[512]{0:T(512)S(1)} %fusion.139) | copy-start | bytes 6148
  393.8 42.8 %copy-start.227 = (f32[512]{0:T(512)}, f32[512]{0:T(512)S(1)}, u32[]{:S(2)}) copy-start(f32[512]{0:T(512)S(1)} %fusion.137) | copy-start | bytes 6148
  394.8 40.6 %copy-start.231 = (f32[512]{0:T(512)}, f32[512]{0:T(512)S(1)}, u32[]{:S(2)}) copy-start(f32[512]{0:T(512)S(1)} %fusion.135) | copy-start | bytes 6148
  395.3 39.0 %copy-start.235 = (f32[512]{0:T(512)}, f32[512]{0:T(512)S(1)}, u32[]{:S(2)}) copy-start(f32[512]{0:T(512)S(1)} %fusion.133) | copy-start | bytes 6148
  396.4 36.7 %copy-start.239 = (f32[512]{0:T(512)}, f32[512]{0:T(512)S(1)}, u32[]{:S(2)}) copy-start(f32[512]{0:T(512)S(1)} %fusion.131) | copy-start | bytes 6148
  396.8 35.1 %copy-start.243 = (f32[512]{0:T(512)}, f32[512]{0:T(512)S(1)}, u32[]{:S(2)}) copy-start(f32[512]{0:T(512)S(1)} %fusion.129) | copy-start | bytes 6148
  397.9 32.7 %copy-start.249 = (f32[512]{0:T(512)}, f32[512]{0:T(512)S(1)}, u32[]{:S(2)}) copy-start(f32[512]{0:T(512)S(1)} %fusion.127) | copy-start | bytes 6148
  462.3 77.0 %copy-start.87 = (bf16[512,768]{0,1:T(8,128)(2,1)}, bf16[512,768]{0,1:T(8,128)(2,1)S(1)}, u32[]{:S(2)}) copy-start(bf16[512,768]{0,1:T(8,128)(2,1)S(1)} %fusion.51) | copy-start | bytes 2359300
  462.9 78.5 %copy-start.89 = (bf16[512,768]{0,1:T(8,128)(2,1)}, bf16[512,768]{0,1:T(8,128)(2,1)S(1)}, u32[]{:S(2)}) copy-start(bf16[512,768]{0,1:T(8,128)(2,1)S(1)} %fusion.49) | copy-start | bytes 2359300
  648.9 8.6 copy-start.27
  648.9 8.6 copy-start.182
  648.9 8.6 copy-start.200
  648.9 68.0 %all-to-all-start.4 = ((bf16[32,64,1024]{2,1,0:T(8,128)(2,1)}), bf16[32,64,1024]{2,1,0:T(8,128)(2,1)}, u32[]{:S(2)}, u32[]{:S(2)}) async-start(bf16[32,64,1024]{2,1,0:T(8,128)(2,1)} %bitcast.443), calls=%async_computation.4 | async-start | bytes 8388608 | tf_op jit(solution)/shard_map/all_to_all | solution.py:140
  716.9 12.4 %copy-start.116 = (bf16[512,768]{0,1:T(8,128)(2,1)S(1)}, bf16[512,768]{0,1:T(8,128)(2,1)}, u32[]{:S(2)}) copy-start(bf16[512,768]{0,1:T(8,128)(2,1)} %fusion.45) | copy-start | bytes 2359300
  716.9 58.1 %all-to-all-start.6 = ((bf16[32,64,1024]{2,1,0:T(8,128)(2,1)}), bf16[32,64,1024]{2,1,0:T(8,128)(2,1)}, u32[]{:S(2)}, u32[]{:S(2)}) async-start(bf16[32,64,1024]{2,1,0:T(8,128)(2,1)} %bitcast.444), calls=%async_computation.6 | async-start | bytes 8388608 | tf_op jit(solution)/shard_map/all_to_all | solution.py:147
  724.7 6.6 copy-start.11
  775.0 50.8 %all-to-all-start.5 = ((bf16[32,64,1024]{2,0,1:T(8,128)(2,1)}), bf16[32,64,1024]{2,0,1:T(8,128)(2,1)}, u32[]{:S(2)}, u32[]{:S(2)}) async-start(bf16[32,64,1024]{2,0,1:T(8,128)(2,1)} %copy.381), calls=%async_computation.5 | async-start | bytes 8388608 | tf_op jit(solution)/shard_map/all_to_all | solution.py:139
  779.9 6.7 copy-start.122
  825.8 117.8 %all-to-all-start.7 = ((bf16[32,64,1024]{2,0,1:T(8,128)(2,1)}), bf16[32,64,1024]{2,0,1:T(8,128)(2,1)}, u32[]{:S(2)}, u32[]{:S(2)}) async-start(bf16[32,64,1024]{2,0,1:T(8,128)(2,1)} %copy.387), calls=%async_computation.7 | async-start | bytes 8388608 | tf_op jit(solution)/shard_map/all_to_all | solution.py:146
  840.5 6.6 copy-start.70
  840.5 6.6 copy-start.71
  840.5 6.6 copy-start.72
  931.4 7.8 copy-start.185
  931.4 7.8 copy-start.256
  (201 other events, 500.1 us)
where the time goes:
time: 976 us; the launch traced here: 964 us
  local copies, waits for them, and re-layouts  370 us (38%)
  matrix products  334 us (34%)
  waiting for transfers between devices  108 us (11%)
  blocking collectives  67 us (7%)
  starting transfers between devices  53.3 us (5%)
  other arithmetic  28.8 us (3%)
    unnamed x528, local copies, waits for them, and re-layouts  126 us
    dot_general x64, matrix products, contract_last(): lax.dot_general(left, right, (((1,), (1,)), ((), ())), preferred_element_...  121 us
    dot_general x64, matrix products, contract_first(): lax.dot_general(left, right, (((0,), (0,)), ((), ())), preferred_element_...  93.7 us
    psum x1, blocking collectives, local(): grad_gate = lax.psum(gate_part, 'seq')  67 us
    all_to_all x1, waiting for transfers between devices, local(): lax.all_to_all(latent_keys[send_index], 'seq', split_axis=0, concat_axis=...  47.4 us
    dot_general x32, matrix products, local(): jnp.dot(weights_low, value_head, preferred_element_type=jnp.float32)  41.6 us
    dot_general x32, matrix products, local(): jnp.dot(grad_scores, key_head, preferred_element_type=jnp.float32)  35.5 us
    all_to_all x1, waiting for transfers between devices, local(): lax.all_to_all(part_values, 'seq', split_axis=0, concat_axis=0, tiled=True)  30.1 us
  transfers between devices with their start and end apart: 8, of which 4 were waited for; matrix products, arithmetic and copies ran while one was open for 38% of the time, Pallas kernels for 0%

commit v1 on v0

v1 whole, which is shorter than its diff:
```python
import math

import jax
import jax.numpy as jnp
from jax import lax
from jax.experimental import pallas as pl
from jax.experimental.pallas import tpu as pltpu
from jax.sharding import PartitionSpec as P

HD = 128
LAT = 64
PART = 16
DOC = 32
DOCS = 8
ATT = 12
BLK = 512
ROWS = 2048
HEADS = 4
BLOCKS = 8
HALF = HEADS * HD
KEYS = ATT * LAT
SCALE = 1.0 / math.sqrt(HD)
EXP_SCALE = math.log2(math.e) / math.sqrt(HD)
MESH = pl.DeviceIdType.MESH
f32, bf16, i32 = jnp.float32, jnp.bfloat16, jnp.int32


def contract_last(left, right):
    return lax.dot_general(left, right, (((1,), (1,)), ((), ())), preferred_element_type=f32)


def dot(left, right):
    return jnp.dot(left, right, preferred_element_type=f32)


def kernel(
    slot_ref, lists_ref, q_hbm, cot_hbm, lk, lv, gate_ref,
    out_hbm, gq_hbm, gk_out, gv_out, gate_out,
    own_slot, own_doc, inverse,
    z_send, z_recv, y_recv, x_recv, q_work, c_work, k_all, v_all, k_blk, v_blk,
    k_term, v_term, part, bx_recv, by_send, by_recv, bz_recv,
    g_part, g_x, g_row, g_y, g_all,
    zs, zr, ys, yr, xs, xr, bxs, bxr, bys, byr, bzs, bzr,
    til, tis, tir, tol, tos, tor, gxs, gxr, gys, gyr, gcs, gcr,
):
    seq = lax.axis_index("seq")
    z = lax.axis_index("vis")
    c = seq % 2
    x = (seq // 2) % 4
    y = seq // 8

    def at_z(k):
        return (y * 8 + x * 2 + (c + k) % 2, (z + k // 2) % 4)

    def at_y(k):
        return (((y + k) % 4) * 8 + x * 2 + c, z)

    def at_x(k):
        return (y * 8 + ((x + k) % 4) * 2 + c, z)

    sibling = at_z(1)

    def copy(src, dst, send, recv, device, k):
        if k == 0:
            return pltpu.make_async_copy(src, dst, recv)
        return pltpu.make_async_remote_copy(
            src_ref=src, dst_ref=dst, send_sem=send, recv_sem=recv, device_id=device, device_id_type=MESH
        )

    def z_copy(h, k):
        to = ((z + k // 2) % 4) * 2 + (c + k) % 2
        return copy(
            z_send.at[h, to], z_recv.at[h, :, c, :, pl.ds(pl.multiple_of(z * PART, PART), PART), :],
            zs.at[h, k], zr.at[h, k], at_z(k), k)

    def y_copy(h, k):
        return copy(
            z_recv.at[h, pl.ds(2 * ((y + k) % 4), 2)], y_recv.at[h, :, pl.ds(2 * y, 2)],
            ys.at[h, k], yr.at[h, k], at_y(k), k)

    def x_copy(h, k):
        return copy(
            y_recv.at[h, ((x + k) % 4) // 2], x_recv.at[h, pl.ds(x * 8, 8)],
            xs.at[h, k], xr.at[h, k], at_x(k), k)

    def bx_copy(h, k):
        return copy(
            part.at[h, pl.ds(((x + k) % 4) * 8, 8)], bx_recv.at[h, x],
            bxs.at[h, k], bxr.at[h, k], at_x(k), k)

    def by_copy(h, k):
        return copy(
            by_send.at[h, :, (y + k) % 4], by_recv.at[h, pl.ds(2 * y, 2)],
            bys.at[h, k], byr.at[h, k], at_y(k), k)

    def bz_copy(h, k):
        to_z = (z + k // 2) % 4
        return copy(
            by_recv.at[h, :, (c + k) % 2, :, pl.ds(pl.multiple_of(to_z * PART, PART), PART), :],
            bz_recv.at[h, z * 2 + c], bzs.at[h, k], bzr.at[h, k], at_z(k), k)

    def columns(half, h):
        return pl.ds(pl.multiple_of(half * HALF + h * HD, HD), HD)

    def text_local(h):
        return [
            pltpu.make_async_copy(src.at[:, columns(c, h)], dst.at[h, pl.ds(0, ROWS)], til.at[h, i])
            for i, (src, dst) in enumerate(((q_hbm, q_work), (cot_hbm, c_work)))]

    def text_remote(h):
        return [
            copy(src.at[:, columns(1 - c, h)], dst.at[h, pl.ds(ROWS, ROWS)],
                 tis.at[h, i], tir.at[h, i], sibling, 1)
            for i, (src, dst) in enumerate(((q_hbm, q_work), (cot_hbm, c_work)))]

    def result_local(h):
        return [
            pltpu.make_async_copy(src.at[h, pl.ds(0, ROWS)], dst.at[:, columns(c, h)], tol.at[h, i])
            for i, (src, dst) in enumerate(((q_work, gq_hbm), (c_work, out_hbm)))]

    def result_remote(h):
        return [
            copy(src.at[h, pl.ds(ROWS, ROWS)], dst.at[:, columns(c, h)],
                 tos.at[h, i], tor.at[h, i], sibling, 1)
            for i, (src, dst) in enumerate(((q_work, gq_hbm), (c_work, out_hbm)))]

    def start(copies):
        for one in copies:
            one.start()

    def arrive(make, h, count):
        make(h, 0).wait()
        for k in range(1, count):
            make(h, k).wait_recv()

    def sent(make, h, count):
        for k in range(1, count):
            make(h, k).wait_send()

    @pl.loop(0, HEADS)
    def _(h):
        start(text_local(h))

    barrier = pltpu.get_barrier_semaphore()
    partners = [at_z(k) for k in range(1, 8)] + [at_y(k) for k in range(1, 4)] + [at_x(k) for k in range(1, 4)]
    for one in partners:
        pl.semaphore_signal(barrier, inc=1, device_id=one, device_id_type=MESH)

    slots = []
    for d in range(DOCS):
        def look(i, found, d=d):
            at = slot_ref[d * DOC + i]
            return found + jnp.where(at // 8 == seq, at % 8, 0)
        slots.append(lax.fori_loop(0, DOC, look, jnp.int32(0), unroll=True))
        own_slot[d] = slots[d]
    for j in range(DOCS):
        doc = jnp.int32(0)
        for d in range(DOCS):
            doc = jnp.where(slots[d] == j, d, doc)
        own_doc[j] = doc

    @pl.loop(0, DOCS)
    def _(d):
        at = own_slot[d]
        for i, src in enumerate((lk, lv)):
            row = src[at]
            for to in range(8):
                for h in range(HEADS):
                    low = (to * HEADS + h) * HD
                    z_send[h, to, d, i] = row[:, low:low + HD]

    pl.semaphore_wait(barrier, len(partners))

    @pl.loop(0, HEADS)
    def _(h):
        for k in range(8):
            z_copy(h, k).start()

    @pl.loop(0, HEADS)
    def _(h):
        start(text_remote(h))

    def block_row(b):
        own = seq * 4 + b
        return jnp.where(b < 4, own, (seq + 1 - 2 * c) * 4 + b - 4)

    def place(b, a):
        owner = slot_ref[lists_ref[block_row(b), a]] // 8
        return ((owner // 2) % 4) * 8 + (owner // 8) * 2 + owner % 2

    @pl.loop(0, BLOCKS)
    def _(b):
        places = [place(b, a) for a in range(ATT)]

        @pl.loop(0, DOC)
        def _(p):
            found = jnp.int32(ATT)
            for a in range(ATT):
                found = jnp.where(places[a] == p, a, found)
            inverse[b, p] = found

    k_term[:, ATT] = jnp.zeros((BLOCKS, LAT, HD), f32)
    v_term[:, ATT] = jnp.zeros((BLOCKS, LAT, HD), f32)
    v_blk[:, HD:] = jnp.ones((KEYS, HD), bf16)
    g_part[...] = jnp.zeros((8, HD), f32)

    @pl.loop(0, HEADS + 1)
    def _(t):
        @pl.when(t < HEADS)
        def _():
            arrive(z_copy, t, 8)
            start([y_copy(t, k) for k in range(4)])

        @pl.when(t >= 1)
        def _():
            arrive(y_copy, t - 1, 4)
            start([x_copy(t - 1, k) for k in range(4)])

    def fold(h):
        arrive(bx_copy, h, 4)

        @pl.loop(0, 8)
        def _(i):
            for p in range(2):
                both = bx_recv[h, 2 * p, i].astype(f32) + bx_recv[h, 2 * p + 1, i].astype(f32)
                by_send[h, p, i // 2, i % 2] = both.astype(bf16)

        start([by_copy(h, k) for k in range(4)])

    def scatter(h):
        arrive(by_copy, h, 4)
        start([bz_copy(h, k) for k in range(8)])

    @pl.loop(0, HEADS)
    def _(h):
        arrive(x_copy, h, 4)
        for one in text_local(h):
            one.wait()
        for one in text_remote(h):
            one.wait_recv()
        k_all[...] = x_recv[h, :, 0]
        v_all[...] = x_recv[h, :, 1]
        gate = jnp.tanh(gate_ref[c * HEADS + h])

        def block(b, total):
            for a in range(ATT):
                at = place(b, a)
                k_blk[a * LAT:(a + 1) * LAT] = k_all[at]
                v_blk[a * LAT:(a + 1) * LAT, :HD] = v_all[at]
            keys = k_blk[...]
            values = v_blk[...]
            rows = pl.ds(pl.multiple_of(b * BLK, BLK), BLK)
            queries = q_work[h, rows]
            cot = c_work[h, rows].astype(f32)
            grad_attn = (cot * gate).astype(bf16)
            scores = contract_last(queries, keys)
            top = jnp.max(scores, axis=1, keepdims=True)
            raised = jnp.exp2((scores - top) * EXP_SCALE)
            raised_low = raised.astype(bf16)
            summed = dot(raised_low, values)
            share = 1.0 / summed[:, HD:]
            attended = summed[:, :HD] * share
            c_work[h, rows] = (attended * gate).astype(bf16)
            total = total + jnp.sum((cot * attended).reshape(BLK // 8, 8, HD), axis=0)
            row_dot = jnp.sum(grad_attn.astype(f32) * attended, axis=1, keepdims=True)
            grad_weights = contract_last(grad_attn, values[:, :HD])
            grad_scores = (raised * (grad_weights - row_dot)).astype(bf16)
            scaled = share * SCALE
            q_work[h, rows] = (dot(grad_scores, keys) * scaled).astype(bf16)
            query_share = (queries.astype(f32) * scaled).astype(bf16)
            grad_share = (grad_attn.astype(f32) * share).astype(bf16)
            k_term[b, :ATT] = dot(query_share.T, grad_scores).T.reshape(ATT, LAT, HD)
            v_term[b, :ATT] = dot(grad_share.T, raised_low).T.reshape(ATT, LAT, HD)
            return total

        total = lax.fori_loop(0, BLOCKS, block, jnp.zeros((8, HD), f32), unroll=UNROLL)
        g_part[pl.ds(h, 1)] = jnp.sum(total, axis=0, keepdims=True) * (1.0 - gate * gate)

        start(result_local(h))
        start(result_remote(h))

        @pl.loop(0, DOC)
        def _(p):
            key_sum = k_term[0, inverse[0, p]]
            value_sum = v_term[0, inverse[0, p]]
            for b in range(1, BLOCKS):
                key_sum = key_sum + k_term[b, inverse[b, p]]
                value_sum = value_sum + v_term[b, inverse[b, p]]
            part[h, p, 0] = key_sum.astype(bf16)
            part[h, p, 1] = value_sum.astype(bf16)

        start([bx_copy(h, k) for k in range(4)])

        @pl.when(h >= 1)
        def _():
            fold(h - 1)

        @pl.when(h >= 2)
        def _():
            scatter(h - 2)

    def gx_copy(k):
        return copy(g_part, g_x.at[x], gxs.at[k], gxr.at[k], at_x(k), k)

    def gy_copy(k):
        return copy(g_row, g_y.at[y], gys.at[k], gyr.at[k], at_y(k), k)

    def gc_copy(k):
        return copy(g_row, g_all.at[c], gcs.at[k], gcr.at[k], sibling, k)

    start([gx_copy(k) for k in range(4)])
    scatter(HEADS - 2)
    gx_copy(0).wait()
    for k in range(1, 4):
        gx_copy(k).wait()
    g_row[...] = (g_x[0] + g_x[1]) + (g_x[2] + g_x[3])
    start([gy_copy(k) for k in range(4)])
    fold(HEADS - 1)
    gy_copy(0).wait()
    for k in range(1, 4):
        gy_copy(k).wait()
    g_row[...] = (g_y[0] + g_y[1]) + (g_y[2] + g_y[3])
    start([gc_copy(k) for k in range(2)])
    scatter(HEADS - 1)
    gc_copy(0).wait()
    gc_copy(1).wait()
    for half in range(2):
        gate_out[half * HEADS:(half + 1) * HEADS] = g_all[half, :HEADS]

    @pl.loop(0, HEADS)
    def _(h):
        sent(z_copy, h, 8)
        sent(y_copy, h, 4)
        sent(x_copy, h, 4)
        sent(bx_copy, h, 4)
        sent(by_copy, h, 4)
        for one in text_remote(h):
            one.wait_send()
        for one in result_local(h):
            one.wait()
        for one in result_remote(h):
            one.wait()

    @pl.loop(0, HEADS)
    def _(h):
        arrive(bz_copy, h, 8)
        sent(bz_copy, h, 8)

    @pl.loop(0, DOCS)
    def _(j):
        d = own_doc[j]
        for h in range(HEADS):
            for source in range(8):
                low = (source * HEADS + h) * HD
                gk_out[j, :, low:low + HD] = bz_recv[h, source, d, 0]
                gv_out[j, :, low:low + HD] = bz_recv[h, source, d, 1]


UNROLL = 1


def local(queries, latent_keys, latent_values, gate_vector, cotangent, image_slot, image_lists):
    smem = pl.BlockSpec(memory_space=pltpu.SMEM)
    vmem = pl.BlockSpec(memory_space=pltpu.VMEM)
    hbm = pl.BlockSpec(memory_space=pl.ANY)
    dma = pltpu.SemaphoreType.DMA
    outs = pl.pallas_call(
        kernel,
        out_shape=[
            jax.ShapeDtypeStruct(queries.shape, bf16),
            jax.ShapeDtypeStruct(queries.shape, bf16),
            jax.ShapeDtypeStruct(latent_keys.shape, bf16),
            jax.ShapeDtypeStruct(latent_keys.shape, bf16),
            jax.ShapeDtypeStruct((2 * HEADS, HD), f32),
        ],
        in_specs=[smem, smem, hbm, hbm, vmem, vmem, vmem],
        out_specs=[hbm, hbm, vmem, vmem, vmem],
        scratch_shapes=[
            pltpu.SMEM((DOCS,), i32),
            pltpu.SMEM((DOCS,), i32),
            pltpu.SMEM((BLOCKS, DOC), i32),
            pltpu.VMEM((HEADS, 8, DOCS, 2, PART, HD), bf16),
            pltpu.VMEM((HEADS, DOCS, 2, 2, LAT, HD), bf16),
            pltpu.VMEM((HEADS, 2, 8, 2, LAT, HD), bf16),
            pltpu.VMEM((HEADS, DOC, 2, LAT, HD), bf16),
            pltpu.VMEM((HEADS, 2 * ROWS, HD), bf16),
            pltpu.VMEM((HEADS, 2 * ROWS, HD), bf16),
            pltpu.VMEM((DOC, LAT, HD), bf16),
            pltpu.VMEM((DOC, LAT, HD), bf16),
            pltpu.VMEM((KEYS, HD), bf16),
            pltpu.VMEM((KEYS, 2 * HD), bf16),
            pltpu.VMEM((BLOCKS, ATT + 1, LAT, HD), f32),
            pltpu.VMEM((BLOCKS, ATT + 1, LAT, HD), f32),
            pltpu.VMEM((HEADS, DOC, 2, LAT, HD), bf16),
            pltpu.VMEM((HEADS, 4, 8, 2, LAT, HD), bf16),
            pltpu.VMEM((HEADS, 2, 4, 2, 2, LAT, HD), bf16),
            pltpu.VMEM((HEADS, DOCS, 2, 2, LAT, HD), bf16),
            pltpu.VMEM((HEADS, 8, DOCS, 2, PART, HD), bf16),
            pltpu.VMEM((8, HD), f32),
            pltpu.VMEM((4, 8, HD), f32),
            pltpu.VMEM((8, HD), f32),
            pltpu.VMEM((4, 8, HD), f32),
            pltpu.VMEM((2, 8, HD), f32),
            dma((HEADS, 8)), dma((HEADS, 8)), dma((HEADS, 4)), dma((HEADS, 4)), dma((HEADS, 4)), dma((HEADS, 4)),
            dma((HEADS, 4)), dma((HEADS, 4)), dma((HEADS, 4)), dma((HEADS, 4)), dma((HEADS, 8)), dma((HEADS, 8)),
            dma((HEADS, 2)), dma((HEADS, 2)), dma((HEADS, 2)), dma((HEADS, 2)), dma((HEADS, 2)), dma((HEADS, 2)),
            dma((4,)), dma((4,)), dma((4,)), dma((4,)), dma((2,)), dma((2,)),
        ],
        compiler_params=pltpu.CompilerParams(
            collective_id=0, has_side_effects=True, vmem_limit_bytes=60 * 2**20
        ),
        name="attention",
    )(image_slot, image_lists, queries, cotangent, latent_keys, latent_values, gate_vector.reshape(2 * HEADS, 1, HD))
    gated, grad_queries, grad_keys, grad_values, grad_gate = outs
    return gated, grad_queries, grad_keys, grad_values, grad_gate.reshape(-1)


def solution(mesh):
    text, latents = P("seq", "vis"), P("seq", "vis", None)
    return jax.shard_map(
        local,
        mesh=mesh,
        in_specs=(text, latents, latents, P("vis"), text, P(), P()),
        out_specs=(text, text, latents, latents, P("vis")),
        check_vma=False,
    )
```

time: 976 us -> 161 us (0.16); the launches traced: 964 us -> 161 us
  local copies, waits for them, and re-layouts: 370 us -> 10.9 us
  matrix products: 334 us -> 0 us
  Pallas kernels: 0 us -> 149 us
  waiting for transfers between devices: 108 us -> 0 us
  blocking collectives: 67 us -> 0 us
  starting transfers between devices: 53.3 us -> 0 us
  other arithmetic: 28.8 us -> 0 us
    dot_general x202 -> x0, matrix products: 334 us -> none  [the longest x64 121 us: contract_last(): lax.dot_general(left, right, (((1,), (1,)), ((), ())), preferred_element_...]
    pallas_call x0 -> x1, Pallas kernels: none -> 149 us  [local(): pl.pallas_call(kernel, out_shape=[jax.ShapeDtypeStruct(queries.shape, bf1...]
    all_to_all x12 -> x0, local copies, waits for them, and re-layouts: 144 us -> none  [the longest x2 26.2 us: local(): lax.all_to_all(lax.all_to_all(latent_keys[send_index], 'seq', split_axis=...]
    unnamed x528 -> x14, local copies, waits for them, and re-layouts: 126 us -> 10.9 us
    all_to_all x8 -> x0, waiting for transfers between devices: 108 us -> none  [the longest x1 47.4 us: local(): lax.all_to_all(latent_keys[send_index], 'seq', split_axis=0, concat_axis=...]
    psum x1 -> x0, blocking collectives: 67 us -> none  [local(): grad_gate = lax.psum(gate_part, 'seq')]
    all_to_all x8 -> x0, starting transfers between devices: 53.3 us -> none  [the longest x1 8.77 us: local(): lax.all_to_all(latent_keys[send_index], 'seq', split_axis=0, concat_axis=...]
    gather x12 -> x0, local copies, waits for them, and re-layouts: 36 us -> none  [the longest x4 16.3 us: local(): value_block = fetched_values[positions].reshape(ATT * LAT, head_cols)]
  transfers between devices with their start and end apart: 8 -> 0, of which waited for: 4 -> 0; matrix products, arithmetic and copies ran while one was open for 38% -> 0% of each run, Pallas kernels for 0% -> 0%
where the time goes in v1:
time: 161 us
  Pallas kernels  149 us (93%)
  local copies, waits for them, and re-layouts  10.9 us (7%)
    pallas_call x1, Pallas kernels, local(): pl.pallas_call(kernel, out_shape=[jax.ShapeDtypeStruct(queries.shape, bf1...  149 us
    unnamed x14, local copies, waits for them, and re-layouts  10.9 us

profile of v1, /device:TPU:1, one launch (start us, length us, event | category | flops | bytes accessed | tf_op | source)
XLA Modules:
  0.0 160.9 jit_solution(13462847308649585449)
XLA Ops:
  0.6 1.4 copy.12.lists_ref
  2.1 149.3 %attention.1 = (bf16[2048,1024]{1,0:T(8,128)(2,1)}, bf16[2048,1024]{1,0:T(8,128)(2,1)}, bf16[8,16,4096]{2,1,0:T(8,128)(2,1)}, bf16[8,16,4096]{2,1,0:T(8,128)(2,1)}, f32[8,128]{1,0:T(8,128)}) custom-call(s32[256]{0:T(256)} %slot_ref.1, s32[128,12]{1,0:T(8,128)} %copy.12.lists_ref, bf16[2048,1024]{1,0:T(8,128)(2,1)} %q_hbm.1, bf16[2048,1024]{1,0:T(8,128)(2,1)} %cot_hbm.1, ...), custom_call_target="tpu_custom_call" | custom-call | tf_op jit(solution)/shard_map/attention/pallas_call | solution.py:367
  151.3 0.0 copy-start
  151.3 4.8 %copy.18 = bf16[2048,1024]{1,0:T(8,128)(2,1)} copy(bf16[2048,1024]{1,0:T(8,128)(2,1)} %get-tuple-element.20) | data formatting | bytes 8388608
  156.2 0.0 copy-done
  156.2 0.0 copy-start.2
  156.2 0.0 copy-start.1
  156.2 2.1 %copy.19 = bf16[2048,1024]{1,0:T(8,128)(2,1)} copy(bf16[2048,1024]{1,0:T(8,128)(2,1)S(1)} %copy-done) | data formatting | bytes 8388608
  158.3 0.0 copy-done.2
  158.3 0.0 copy-start.3
  158.3 1.0 copy.20
  159.3 0.0 copy-done.1
  159.3 1.0 copy.21
  160.3 0.0 copy-done.3
  160.3 0.6 copy.22
Async XLA Ops:
  151.3 4.8 %copy-start = (bf16[2048,1024]{1,0:T(8,128)(2,1)S(1)}, bf16[2048,1024]{1,0:T(8,128)(2,1)}, u32[]{:S(2)}) copy-start(bf16[2048,1024]{1,0:T(8,128)(2,1)} %get-tuple-element.21) | copy-start | bytes 12582916
  156.2 2.1 %copy-start.2 = (bf16[8,16,4096]{2,1,0:T(8,128)(2,1)S(1)}, bf16[8,16,4096]{2,1,0:T(8,128)(2,1)}, u32[]{:S(2)}) copy-start(bf16[8,16,4096]{2,1,0:T(8,128)(2,1)} %get-tuple-element.22) | copy-start | bytes 3145732
  156.2 3.1 %copy-start.1 = (bf16[8,16,4096]{2,1,0:T(8,128)(2,1)S(1)}, bf16[8,16,4096]{2,1,0:T(8,128)(2,1)}, u32[]{:S(2)}) copy-start(bf16[8,16,4096]{2,1,0:T(8,128)(2,1)} %get-tuple-element.23) | copy-start | bytes 3145732
  158.3 1.9 %copy-start.3 = (f32[8,128]{1,0:T(8,128)S(1)}, f32[8,128]{1,0:T(8,128)}, u32[]{:S(2)}) copy-start(f32[8,128]{1,0:T(8,128)} %get-tuple-element.14) | copy-start | bytes 12292

commit v2 on v1

v2 whole, which is shorter than its diff:
```python
import math

import jax
import jax.numpy as jnp
from jax import lax
from jax.experimental import pallas as pl
from jax.experimental.pallas import tpu as pltpu
from jax.sharding import PartitionSpec as P

HD = 128
LAT = 64
PART = 16
DOC = 32
DOCS = 8
ATT = 12
BLK = 512
ROWS = 2048
HEADS = 4
BLOCKS = 8
HALF = HEADS * HD
NEAR = 32
KEYS = ATT * LAT
SCALE = 1.0 / math.sqrt(HD)
EXP_SCALE = math.log2(math.e) / math.sqrt(HD)
MESH = pl.DeviceIdType.MESH
f32, bf16, i32 = jnp.float32, jnp.bfloat16, jnp.int32


def contract_last(left, right):
    return lax.dot_general(left, right, (((1,), (1,)), ((), ())), preferred_element_type=f32)


def dot(left, right):
    return jnp.dot(left, right, preferred_element_type=f32)


def kernel(
    slot_ref, lists_ref, q_hbm, cot_hbm, lk_hbm, lv_hbm, gate_ref,
    out_hbm, gq_hbm, gk_out, gv_out, gate_out,
    own_slot, own_doc, inverse,
    lk, lv, near_send, near_recv, x_recv, q_work, c_work, k_all, v_all, k_blk, v_blk,
    k_term, v_term, bx_recv, back_send, back_recv,
    g_part, g_x, g_row, g_y, g_all,
    ns, nr, xs, xr, bxs, bxr, bs, br,
    lr, til, tis, tir, tol, tos, tor, gxs, gxr, gys, gyr, gcs, gcr,
):
    seq = lax.axis_index("seq")
    z = lax.axis_index("vis")
    c = seq % 2
    x = (seq // 2) % 4
    y = seq // 8

    def at_near(g, k):
        return (((y + g) % 4) * 8 + x * 2 + (c + k) % 2, (z + k // 2) % 4)

    def at_x(k):
        return (y * 8 + ((x + k) % 4) * 2 + c, z)

    sibling = at_near(0, 1)

    def copy(src, dst, send, recv, device, k):
        if k == 0:
            return pltpu.make_async_copy(src, dst, recv)
        return pltpu.make_async_remote_copy(
            src_ref=src, dst_ref=dst, send_sem=send, recv_sem=recv, device_id=device, device_id_type=MESH
        )

    def near_copy(h, g, k, remote):
        to_z, to_c, to_y = (z + k // 2) % 4, (c + k) % 2, (y + g) % 4
        src = near_send.at[h, to_z * 2 + to_c, pl.ds(2 * to_y, 2)]
        dst = near_recv.at[h, :, y * 2 + c, :, pl.ds(pl.multiple_of(z * PART, PART), PART), :]
        if not remote:
            return pltpu.make_async_copy(src, dst, nr.at[h, g])
        return copy(src, dst, ns.at[h, g, k], nr.at[h, g], at_near(g, k), 1)

    def x_copy(h, g, k):
        rows = 2 * ((y + 4 - g) % 4)
        return copy(
            near_recv.at[h, ((x + k) % 4) // 2, pl.ds(rows, 2)], x_recv.at[h, pl.ds(x * 8 + rows, 2)],
            xs.at[h, g, k], xr.at[h, g, k], at_x(k), k)

    def bx_copy(h, g, k):
        rows = 2 * ((y + g) % 4)
        return copy(
            x_recv.at[h, pl.ds(((x + k) % 4) * 8 + rows, 2)], bx_recv.at[h, x, pl.ds(rows, 2)],
            bxs.at[h, g, k], bxr.at[h, g, k], at_x(k), k)

    def back_copy(h, g, k, remote):
        to_z, to_c, to_y = (z + k // 2) % 4, (c + k) % 2, (y + g) % 4
        src = back_send.at[h, :, to_y, to_c, :, pl.ds(pl.multiple_of(to_z * PART, PART), PART), :]
        dst = back_recv.at[h, z * 2 + c, pl.ds(2 * y, 2)]
        if not remote:
            return pltpu.make_async_copy(src, dst, br.at[h])
        return copy(src, dst, bs.at[h, g, k], br.at[h], at_near(g, k), 1)

    def start_group(make, h, g):
        make(h, g, 0, g != 0).start()
        for k in range(1, 8):
            make(h, g, k, True).start()

    def sent_group(make, h, g):
        if g != 0:
            make(h, g, 0, True).wait_send()
        for k in range(1, 8):
            make(h, g, k, True).wait_send()

    def group_arrive(make, h, g):
        make(h, g, 0).wait()
        for k in range(1, 4):
            make(h, g, k).wait_recv()

    def group_sent(make, h, g):
        for k in range(1, 4):
            make(h, g, k).wait_send()

    def columns(half, h):
        return pl.ds(pl.multiple_of(half * HALF + h * HD, HD), HD)

    def text_local(h):
        return [
            pltpu.make_async_copy(src.at[:, columns(c, h)], dst.at[h, pl.ds(0, ROWS)], til.at[h, i])
            for i, (src, dst) in enumerate(((q_hbm, q_work), (cot_hbm, c_work)))]

    def text_remote(h):
        return [
            copy(src.at[:, columns(1 - c, h)], dst.at[h, pl.ds(ROWS, ROWS)],
                 tis.at[h, i], tir.at[h, i], sibling, 1)
            for i, (src, dst) in enumerate(((q_hbm, q_work), (cot_hbm, c_work)))]

    def result_local(h):
        return [
            pltpu.make_async_copy(src.at[h, pl.ds(0, ROWS)], dst.at[:, columns(c, h)], tol.at[h, i])
            for i, (src, dst) in enumerate(((q_work, gq_hbm), (c_work, out_hbm)))]

    def result_remote(h):
        return [
            copy(src.at[h, pl.ds(ROWS, ROWS)], dst.at[:, columns(c, h)],
                 tos.at[h, i], tor.at[h, i], sibling, 1)
            for i, (src, dst) in enumerate(((q_work, gq_hbm), (c_work, out_hbm)))]

    def start(copies):
        for one in copies:
            one.start()

    staged = [
        pltpu.make_async_copy(src, dst, lr.at[i]) for i, (src, dst) in enumerate(((lk_hbm, lk), (lv_hbm, lv)))]
    start(staged)

    @pl.loop(0, HEADS)
    def _(h):
        start(text_local(h))

    barrier = pltpu.get_barrier_semaphore()

    @pl.loop(1, NEAR)
    def _(j):
        pl.semaphore_signal(barrier, inc=1, device_id=at_near(j // 8, j % 8), device_id_type=MESH)

    for k in range(1, 4):
        pl.semaphore_signal(barrier, inc=1, device_id=at_x(k), device_id_type=MESH)

    slots = []
    for d in range(DOCS):
        def look(i, found, d=d):
            at = slot_ref[d * DOC + i]
            return found + jnp.where(at // 8 == seq, at % 8, 0)
        slots.append(lax.fori_loop(0, DOC, look, jnp.int32(0), unroll=True))
        own_slot[d] = slots[d]
    for j in range(DOCS):
        doc = jnp.int32(0)
        for d in range(DOCS):
            doc = jnp.where(slots[d] == j, d, doc)
        own_doc[j] = doc

    for one in staged:
        one.wait()

    @pl.loop(0, DOCS)
    def _(d):
        at = own_slot[d]
        for i, src in enumerate((lk, lv)):
            row = src[at]
            for to in range(8):
                for h in range(HEADS):
                    low = (to * HEADS + h) * HD
                    near_send[h, to, d, i] = row[:, low:low + HD]

    pl.semaphore_wait(barrier, NEAR - 1 + 3)

    def send_out(h):
        for g in (0, 1, 3, 2):
            start_group(near_copy, h, g)

    def block_row(b):
        own = seq * 4 + b
        return jnp.where(b < 4, own, (seq + 1 - 2 * c) * 4 + b - 4)

    def place(b, a):
        owner = slot_ref[lists_ref[a, block_row(b)]] // 8
        return ((owner // 2) % 4) * 8 + (owner // 8) * 2 + owner % 2

    def pass_group(h, g):
        rows = near_recv.at[h, :, pl.ds(2 * ((y + 4 - g) % 4), 2)]
        pltpu.make_async_copy(rows, rows, nr.at[h, g]).wait()
        start([x_copy(h, g, k) for k in range(4)])

    def pass_on(h):
        for g in (0, 1, 3, 2):
            pass_group(h, g)

    start_group(near_copy, 0, 0)
    start_group(near_copy, 0, 1)
    pass_group(0, 0)
    start_group(near_copy, 0, 3)
    pass_group(0, 1)
    start_group(near_copy, 0, 2)
    start(text_remote(0))
    pass_group(0, 3)
    pass_group(0, 2)
    send_out(1)

    @pl.loop(1, HEADS)
    def _(h):
        start(text_remote(h))

    @pl.loop(0, BLOCKS)
    def _(b):
        places = [place(b, a) for a in range(ATT)]

        @pl.loop(0, DOC)
        def _(p):
            found = jnp.int32(ATT)
            for a in range(ATT):
                found = jnp.where(places[a] == p, a, found)
            inverse[b, p] = found

    k_term[:, ATT] = jnp.zeros((BLOCKS, LAT, HD), f32)
    v_term[:, ATT] = jnp.zeros((BLOCKS, LAT, HD), f32)
    v_blk[:, HD:] = jnp.ones((KEYS, HD), bf16)
    g_part[...] = jnp.zeros((8, HD), f32)

    def fold_group(h, g):
        group_arrive(bx_copy, h, g)
        to_y = (y + g) % 4
        for i in range(2):
            for p in range(2):
                both = bx_recv[h, 2 * p, 2 * to_y + i].astype(f32) + bx_recv[h, 2 * p + 1, 2 * to_y + i].astype(f32)
                back_send[h, p, to_y, i] = both.astype(bf16)
        start_group(back_copy, h, g)

    def return_group(h, g):
        start([bx_copy(h, g, k) for k in range(4)])

    def fold(h):
        for g in (2, 1, 3, 0):
            fold_group(h, g)

    @pl.loop(0, HEADS)
    def _(h):
        for g in range(4):
            group_arrive(x_copy, h, g)
        for one in text_local(h):
            one.wait()
        for one in text_remote(h):
            one.wait_recv()
        k_all[...] = x_recv[h, :, 0]
        v_all[...] = x_recv[h, :, 1]
        gate = jnp.tanh(gate_ref[c * HEADS + h])

        def block(b, total):
            @pl.when((h == 0) & (b == 0))
            def _():
                pass_on(1)
                send_out(2)

            @pl.when((h == 0) & (b == 3))
            def _():
                send_out(3)

            @pl.when((h == 0) & (b == 5))
            def _():
                pass_on(2)

            @pl.when((h == 1) & (b == 3))
            def _():
                pass_on(3)

            @pl.when((h >= 2) & (b == 3))
            def _():
                fold(h - 2)

            for a in range(ATT):
                at = place(b, a)
                k_blk[a * LAT:(a + 1) * LAT] = k_all[at]
                v_blk[a * LAT:(a + 1) * LAT, :HD] = v_all[at]
            keys = k_blk[...]
            values = v_blk[...]
            rows = pl.ds(pl.multiple_of(b * BLK, BLK), BLK)
            queries = q_work[h, rows]
            cot = c_work[h, rows].astype(f32)
            grad_attn = (cot * gate).astype(bf16)
            scores = contract_last(queries, keys)
            top = jnp.max(scores, axis=1, keepdims=True)
            raised = jnp.exp2((scores - top) * EXP_SCALE)
            raised_low = raised.astype(bf16)
            summed = dot(raised_low, values)
            share = 1.0 / summed[:, HD:]
            attended = summed[:, :HD] * share
            c_work[h, rows] = (attended * gate).astype(bf16)
            total = total + jnp.sum((cot * attended).reshape(BLK // 8, 8, HD), axis=0)
            row_dot = jnp.sum(grad_attn.astype(f32) * attended, axis=1, keepdims=True)
            grad_weights = contract_last(grad_attn, values[:, :HD])
            grad_scores = (raised * (grad_weights - row_dot)).astype(bf16)
            scaled = share * SCALE
            q_work[h, rows] = (dot(grad_scores, keys) * scaled).astype(bf16)
            query_share = (queries.astype(f32) * scaled).astype(bf16)
            grad_share = (grad_attn.astype(f32) * share).astype(bf16)
            k_term[b, :ATT] = dot(query_share.T, grad_scores).T.reshape(ATT, LAT, HD)
            v_term[b, :ATT] = dot(grad_share.T, raised_low).T.reshape(ATT, LAT, HD)
            return total

        total = lax.fori_loop(0, BLOCKS, block, jnp.zeros((8, HD), f32), unroll=UNROLL)
        g_part[pl.ds(h, 1)] = jnp.sum(total, axis=0, keepdims=True) * (1.0 - gate * gate)

        start(result_local(h))
        start(result_remote(h))

        @pl.loop(0, DOC)
        def _(p):
            key_sum = k_term[0, inverse[0, p]]
            value_sum = v_term[0, inverse[0, p]]
            for b in range(1, BLOCKS):
                key_sum = key_sum + k_term[b, inverse[b, p]]
                value_sum = value_sum + v_term[b, inverse[b, p]]
            x_recv[h, p, 0] = key_sum.astype(bf16)
            x_recv[h, p, 1] = value_sum.astype(bf16)

        return_group(h, 2)
        return_group(h, 1)

        @pl.when(h < HEADS - 1)
        def _():
            return_group(h, 3)
            return_group(h, 0)

    def gx_copy(k):
        return copy(g_part, g_x.at[x], gxs.at[k], gxr.at[k], at_x(k), k)

    def gy_copy(k):
        return copy(g_row, g_y.at[y], gys.at[k], gyr.at[k], at_near(k, 0), k)

    def gc_copy(k):
        return copy(g_row, g_all.at[c], gcs.at[k], gcr.at[k], sibling, k)

    def settle_x():
        for k in range(4):
            gx_copy(k).wait()
        g_row[...] = (g_x[0] + g_x[1]) + (g_x[2] + g_x[3])
        start([gy_copy(k) for k in range(4)])

    def settle_y():
        for k in range(4):
            gy_copy(k).wait()
        g_row[...] = (g_y[0] + g_y[1]) + (g_y[2] + g_y[3])
        start([gc_copy(k) for k in range(2)])

    last = HEADS - 1
    start([gx_copy(k) for k in range(4)])
    fold(last - 1)
    fold_group(last, 2)
    return_group(last, 3)
    fold_group(last, 1)
    return_group(last, 0)
    settle_x()
    fold_group(last, 3)
    settle_y()
    fold_group(last, 0)

    @pl.loop(0, HEADS)
    def _(h):
        for g in range(4):
            sent_group(near_copy, h, g)
            group_sent(x_copy, h, g)
        for one in text_remote(h):
            one.wait_send()

    @pl.loop(0, HEADS)
    def _(h):
        for one in result_local(h):
            one.wait()
        for one in result_remote(h):
            one.wait()

    gc_copy(0).wait()
    gc_copy(1).wait()
    for half in range(2):
        gate_out[half * HEADS:(half + 1) * HEADS] = g_all[half, :HEADS]

    @pl.loop(0, HEADS)
    def _(h):
        for g in range(4):
            group_sent(bx_copy, h, g)
            sent_group(back_copy, h, g)
        pltpu.make_async_copy(back_recv.at[h], back_recv.at[h], br.at[h]).wait()

    @pl.loop(0, DOCS)
    def _(j):
        d = own_doc[j]
        for h in range(HEADS):
            for source in range(8):
                low = (source * HEADS + h) * HD
                gk_out[j, :, low:low + HD] = back_recv[h, source, d, 0]
                gv_out[j, :, low:low + HD] = back_recv[h, source, d, 1]


UNROLL = 1
VMEM = 48


def local(queries, latent_keys, latent_values, gate_vector, cotangent, image_slot, image_lists):
    smem = pl.BlockSpec(memory_space=pltpu.SMEM)
    vmem = pl.BlockSpec(memory_space=pltpu.VMEM)
    hbm = pl.BlockSpec(memory_space=pl.ANY)
    dma = pltpu.SemaphoreType.DMA
    outs = pl.pallas_call(
        kernel,
        out_shape=[
            pltpu.VMEM(queries.shape, bf16),
            pltpu.VMEM(queries.shape, bf16),
            pltpu.VMEM(latent_keys.shape, bf16),
            pltpu.VMEM(latent_keys.shape, bf16),
            pltpu.VMEM((2 * HEADS, HD), f32),
        ],
        in_specs=[smem, smem, hbm, hbm, hbm, hbm, vmem],
        out_specs=[vmem, vmem, vmem, vmem, vmem],
        scratch_shapes=[
            pltpu.SMEM((DOCS,), i32),
            pltpu.SMEM((DOCS,), i32),
            pltpu.SMEM((BLOCKS, DOC), i32),
            pltpu.VMEM((DOCS, PART, 8 * HALF), bf16),
            pltpu.VMEM((DOCS, PART, 8 * HALF), bf16),
            pltpu.VMEM((HEADS, 8, DOCS, 2, PART, HD), bf16),
            pltpu.VMEM((HEADS, 2, 8, 2, LAT, HD), bf16),
            pltpu.VMEM((HEADS, DOC, 2, LAT, HD), bf16),
            pltpu.VMEM((HEADS, 2 * ROWS, HD), bf16),
            pltpu.VMEM((HEADS, 2 * ROWS, HD), bf16),
            pltpu.VMEM((DOC, LAT, HD), bf16),
            pltpu.VMEM((DOC, LAT, HD), bf16),
            pltpu.VMEM((KEYS, HD), bf16),
            pltpu.VMEM((KEYS, 2 * HD), bf16),
            pltpu.VMEM((BLOCKS, ATT + 1, LAT, HD), f32),
            pltpu.VMEM((BLOCKS, ATT + 1, LAT, HD), f32),
            pltpu.VMEM((HEADS, 4, 8, 2, LAT, HD), bf16),
            pltpu.VMEM((HEADS, 2, 4, 2, 2, LAT, HD), bf16),
            pltpu.VMEM((HEADS, 8, DOCS, 2, PART, HD), bf16),
            pltpu.VMEM((8, HD), f32),
            pltpu.VMEM((4, 8, HD), f32),
            pltpu.VMEM((8, HD), f32),
            pltpu.VMEM((4, 8, HD), f32),
            pltpu.VMEM((2, 8, HD), f32),
            dma((HEADS, 4, 8)), dma((HEADS, 4)), dma((HEADS, 4, 4)), dma((HEADS, 4, 4)),
            dma((HEADS, 4, 4)), dma((HEADS, 4, 4)), dma((HEADS, 4, 8)), dma((HEADS,)),
            dma((2,)), dma((HEADS, 2)), dma((HEADS, 2)), dma((HEADS, 2)), dma((HEADS, 2)), dma((HEADS, 2)), dma((HEADS, 2)),
            dma((4,)), dma((4,)), dma((4,)), dma((4,)), dma((2,)), dma((2,)),
        ],
        compiler_params=pltpu.CompilerParams(
            collective_id=0, has_side_effects=True, vmem_limit_bytes=VMEM * 2**20
        ),
        name="attention",
    )(image_slot, image_lists.T, queries, cotangent, latent_keys, latent_values, gate_vector.reshape(2 * HEADS, 1, HD))
    gated, grad_queries, grad_keys, grad_values, grad_gate = outs
    return gated, grad_queries, grad_keys, grad_values, grad_gate.reshape(-1)


def solution(mesh):
    text, latents = P("seq", "vis"), P("seq", "vis", None)
    return jax.shard_map(
        local,
        mesh=mesh,
        in_specs=(text, latents, latents, P("vis"), text, P(), P()),
        out_specs=(text, text, latents, latents, P("vis")),
        check_vma=False,
    )
```

time: 161 us -> 133 us (0.83)
  Pallas kernels: 149 us -> 126 us
  local copies, waits for them, and re-layouts: 10.9 us -> 6.56 us
    pallas_call x1, Pallas kernels: 149 us -> 126 us  [local(): pl.pallas_call(kernel, out_shape=[pltpu.VMEM(queries.shape, bf16), pltpu....]
    unnamed x14 -> x5, local copies, waits for them, and re-layouts: 10.9 us -> 6.56 us
where the time goes in v2:
time: 133 us
  Pallas kernels  126 us (95%)
  local copies, waits for them, and re-layouts  6.56 us (5%)
    pallas_call x1, Pallas kernels, local(): pl.pallas_call(kernel, out_shape=[pltpu.VMEM(queries.shape, bf16), pltpu....  126 us
    unnamed x5, local copies, waits for them, and re-layouts  6.56 us

profile of v2, /device:TPU:1, one launch (start us, length us, event | category | flops | bytes accessed | tf_op | source)
XLA Modules:
  0.0 132.8 jit_solution(1441136844183084993)
XLA Ops:
  0.6 125.6 %attention.1 = (bf16[2048,1024]{1,0:T(8,128)(2,1)S(1)}, bf16[2048,1024]{1,0:T(8,128)(2,1)S(1)}, bf16[8,16,4096]{2,1,0:T(8,128)(2,1)S(1)}, bf16[8,16,4096]{2,1,0:T(8,128)(2,1)S(1)}, f32[8,128]{1,0:T(8,128)S(1)}) custom-call(s32[256]{0:T(256)} %slot_ref.1, s32[12,128]{1,0:T(8,128)} %bitcast.4, bf16[2048,1024]{1,0:T(8,128)(2,1)} %q_hbm.1, ...), custom_call_target="tpu_custom_call" | custom-call | tf_op jit(solution)/shard_map/attention/pallas_call | solution.py:425
  126.2 2.0 %copy.17 = bf16[2048,1024]{1,0:T(8,128)(2,1)} copy(bf16[2048,1024]{1,0:T(8,128)(2,1)S(1)} %get-tuple-element.15) | data formatting | bytes 8388608
  128.2 0.6 copy.21
  128.8 1.0 copy.19
  129.8 1.0 copy.20
  130.8 2.0 %copy.18 = bf16[2048,1024]{1,0:T(8,128)(2,1)} copy(bf16[2048,1024]{1,0:T(8,128)(2,1)S(1)} %get-tuple-element.16) | data formatting | bytes 8388608

commit v3 on v2

--- a/solution.py
+++ b/solution.py
@@ -71,7 +71,7 @@
         dst = near_recv.at[h, :, y * 2 + c, :, pl.ds(pl.multiple_of(z * PART, PART), PART), :]
         if not remote:
             return pltpu.make_async_copy(src, dst, nr.at[h, g])
-        return copy(src, dst, ns.at[h, g, k], nr.at[h, g], at_near(g, k), 1)
+        return copy(src, dst, ns.at[h, g, k if g == 0 else 0], nr.at[h, g], at_near(g, k), 1)
 
     def x_copy(h, g, k):
         rows = 2 * ((y + 4 - g) % 4)
@@ -91,7 +91,7 @@
         dst = back_recv.at[h, z * 2 + c, pl.ds(2 * y, 2)]
         if not remote:
             return pltpu.make_async_copy(src, dst, br.at[h])
-        return copy(src, dst, bs.at[h, g, k], br.at[h], at_near(g, k), 1)
+        return copy(src, dst, bs.at[h, g, k if g == 0 else 0], br.at[h], at_near(g, k), 1)
 
     def start_group(make, h, g):
         make(h, g, 0, g != 0).start()
@@ -99,10 +99,16 @@
             make(h, g, k, True).start()
 
     def sent_group(make, h, g):
-        if g != 0:
-            make(h, g, 0, True).wait_send()
-        for k in range(1, 8):
-            make(h, g, k, True).wait_send()
+        if g == 0:
+            for k in range(1, 8):
+                make(h, g, k, True).wait_send()
+            return
+        to_y = (y + g) % 4
+        if make is near_copy:
+            rows, done = near_send.at[h, :, pl.ds(2 * to_y, 2)], ns.at[h, g, 0]
+        else:
+            rows, done = back_send.at[h, :, to_y], bs.at[h, g, 0]
+        pltpu.make_async_copy(rows, rows, done).wait()
 
     def group_arrive(make, h, g):
         make(h, g, 0).wait()
@@ -142,6 +148,15 @@
         for one in copies:
             one.start()
 
+    barrier = pltpu.get_barrier_semaphore()
+
+    @pl.loop(1, NEAR)
+    def _(j):
+        pl.semaphore_signal(barrier, inc=1, device_id=at_near(j // 8, j % 8), device_id_type=MESH)
+
+    for k in range(1, 4):
+        pl.semaphore_signal(barrier, inc=1, device_id=at_x(k), device_id_type=MESH)
+
     staged = [
         pltpu.make_async_copy(src, dst, lr.at[i]) for i, (src, dst) in enumerate(((lk_hbm, lk), (lv_hbm, lv)))]
     start(staged)
@@ -149,15 +164,6 @@
     @pl.loop(0, HEADS)
     def _(h):
         start(text_local(h))
-
-    barrier = pltpu.get_barrier_semaphore()
-
-    @pl.loop(1, NEAR)
-    def _(j):
-        pl.semaphore_signal(barrier, inc=1, device_id=at_near(j // 8, j % 8), device_id_type=MESH)
-
-    for k in range(1, 4):
-        pl.semaphore_signal(barrier, inc=1, device_id=at_x(k), device_id_type=MESH)
 
     slots = []
     for d in range(DOCS):
@@ -255,10 +261,20 @@
         for g in (2, 1, 3, 0):
             fold_group(h, g)
 
+    group_arrive(x_copy, 0, 0)
+    group_arrive(x_copy, 0, 1)
+    pass_group(1, 0)
+    group_arrive(x_copy, 0, 3)
+    pass_group(1, 1)
+
     @pl.loop(0, HEADS)
     def _(h):
-        for g in range(4):
-            group_arrive(x_copy, h, g)
+        @pl.when(h > 0)
+        def _():
+            for g in (0, 1, 3):
+                group_arrive(x_copy, h, g)
+
+        group_arrive(x_copy, h, 2)
         for one in text_local(h):
             one.wait()
         for one in text_remote(h):
@@ -270,7 +286,8 @@
         def block(b, total):
             @pl.when((h == 0) & (b == 0))
             def _():
-                pass_on(1)
+                pass_group(1, 3)
+                pass_group(1, 2)
                 send_out(2)
 
             @pl.when((h == 0) & (b == 3))
@@ -285,7 +302,7 @@
             def _():
                 pass_on(3)
 
-            @pl.when((h >= 2) & (b == 3))
+            @pl.when((h >= 2) & (b == 5))
             def _():
                 fold(h - 2)
 
@@ -322,26 +339,36 @@
         total = lax.fori_loop(0, BLOCKS, block, jnp.zeros((8, HD), f32), unroll=UNROLL)
         g_part[pl.ds(h, 1)] = jnp.sum(total, axis=0, keepdims=True) * (1.0 - gate * gate)
 
-        start(result_local(h))
-        start(result_remote(h))
-
-        @pl.loop(0, DOC)
-        def _(p):
-            key_sum = k_term[0, inverse[0, p]]
-            value_sum = v_term[0, inverse[0, p]]
-            for b in range(1, BLOCKS):
-                key_sum = key_sum + k_term[b, inverse[b, p]]
-                value_sum = value_sum + v_term[b, inverse[b, p]]
-            x_recv[h, p, 0] = key_sum.astype(bf16)
-            x_recv[h, p, 1] = value_sum.astype(bf16)
-
+        def add_up(g):
+            @pl.loop(0, 8)
+            def _(i):
+                p = (i // 2) * 8 + 2 * ((y + g) % 4) + i % 2
+                key_sum = k_term[0, inverse[0, p]]
+                value_sum = v_term[0, inverse[0, p]]
+                for b in range(1, BLOCKS):
+                    key_sum = key_sum + k_term[b, inverse[b, p]]
+                    value_sum = value_sum + v_term[b, inverse[b, p]]
+                x_recv[h, p, 0] = key_sum.astype(bf16)
+                x_recv[h, p, 1] = value_sum.astype(bf16)
+
+        add_up(2)
         return_group(h, 2)
+        add_up(1)
         return_group(h, 1)
+        add_up(3)
 
         @pl.when(h < HEADS - 1)
         def _():
             return_group(h, 3)
+
+        add_up(0)
+
+        @pl.when(h < HEADS - 1)
+        def _():
             return_group(h, 0)
+
+        start(result_local(h))
+        start(result_remote(h))
 
     def gx_copy(k):
         return copy(g_part, g_x.at[x], gxs.at[k], gxr.at[k], at_x(k), k)
@@ -367,6 +394,20 @@
     last = HEADS - 1
     start([gx_copy(k) for k in range(4)])
     fold(last - 1)
+
+    @pl.loop(0, HEADS)
+    def _(h):
+        for g in range(4):
+            sent_group(near_copy, h, g)
+            group_sent(x_copy, h, g)
+        for one in text_remote(h):
+            one.wait_send()
+
+    @pl.loop(0, last)
+    def _(h):
+        for g in range(4):
+            group_sent(bx_copy, h, g)
+
     fold_group(last, 2)
     return_group(last, 3)
     fold_group(last, 1)
@@ -374,15 +415,13 @@
     settle_x()
     fold_group(last, 3)
     settle_y()
+
+    @pl.loop(0, last)
+    def _(h):
+        for g in range(4):
+            sent_group(back_copy, h, g)
+
     fold_group(last, 0)
-
-    @pl.loop(0, HEADS)
-    def _(h):
-        for g in range(4):
-            sent_group(near_copy, h, g)
-            group_sent(x_copy, h, g)
-        for one in text_remote(h):
-            one.wait_send()
 
     @pl.loop(0, HEADS)
     def _(h):
@@ -391,17 +430,18 @@
         for one in result_remote(h):
             one.wait()
 
+    for g in range(4):
+        group_sent(bx_copy, last, g)
+        sent_group(back_copy, last, g)
+
+    @pl.loop(0, HEADS)
+    def _(h):
+        pltpu.make_async_copy(back_recv.at[h], back_recv.at[h], br.at[h]).wait()
+
     gc_copy(0).wait()
     gc_copy(1).wait()
     for half in range(2):
         gate_out[half * HEADS:(half + 1) * HEADS] = g_all[half, :HEADS]
-
-    @pl.loop(0, HEADS)
-    def _(h):
-        for g in range(4):
-            group_sent(bx_copy, h, g)
-            sent_group(back_copy, h, g)
-        pltpu.make_async_copy(back_recv.at[h], back_recv.at[h], br.at[h]).wait()
 
     @pl.loop(0, DOCS)
     def _(j):
@@ -415,6 +455,29 @@
 
 UNROLL = 1
 VMEM = 48
+
+
+def deliver(*refs):
+    count = len(refs) // 2
+    done = refs[-1]
+    copies = [pltpu.make_async_copy(refs[i], refs[count + i], done.at[i]) for i in range(count)]
+    for one in copies:
+        one.start()
+    for one in copies:
+        one.wait()
+
+
+def delivered(arrays):
+    anywhere = pl.BlockSpec(memory_space=pl.ANY)
+    return pl.pallas_call(
+        deliver,
+        in_specs=[anywhere] * len(arrays),
+        out_specs=[anywhere] * len(arrays),
+        out_shape=[pltpu.HBM(one.shape, one.dtype) for one in arrays],
+        scratch_shapes=[pltpu.SemaphoreType.DMA((len(arrays),))],
+        compiler_params=pltpu.CompilerParams(vmem_limit_bytes=2**20),
+        name="deliver",
+    )(*[pltpu.with_memory_space_constraint(one, pltpu.VMEM) for one in arrays])
 
 
 def local(queries, latent_keys, latent_values, gate_vector, cotangent, image_slot, image_lists):
@@ -468,7 +531,7 @@
         ),
         name="attention",
     )(image_slot, image_lists.T, queries, cotangent, latent_keys, latent_values, gate_vector.reshape(2 * HEADS, 1, HD))
-    gated, grad_queries, grad_keys, grad_values, grad_gate = outs
+    gated, grad_queries, grad_keys, grad_values, grad_gate = delivered(outs)
     return gated, grad_queries, grad_keys, grad_values, grad_gate.reshape(-1)
 
 

time: 133 us -> 129 us (0.970)
  local copies, waits for them, and re-layouts: 6.56 us -> 0 us
  Pallas kernels: 126 us -> 128 us
    unnamed x5 -> x0, local copies, waits for them, and re-layouts: 6.56 us -> none
    pallas_call x0 -> x1, Pallas kernels: none -> 3.98 us  [delivered(): pl.pallas_call(deliver, in_specs=[anywhere] * len(arrays), out_specs=[any...]
where the time goes in v3:
time: 129 us
  Pallas kernels  128 us (99%)
    pallas_call x1, Pallas kernels, local(): pl.pallas_call(kernel, out_shape=[pltpu.VMEM(queries.shape, bf16), pltpu....  124 us
    pallas_call x1, Pallas kernels, delivered(): pl.pallas_call(deliver, in_specs=[anywhere] * len(arrays), out_specs=[any...  3.98 us

profile of v3, /device:TPU:1, one launch (start us, length us, event | category | flops | bytes accessed | tf_op | source)
XLA Modules:
  0.0 128.9 jit_solution(4459299510319758)
XLA Ops:
  0.6 124.3 %attention.1 = (bf16[2048,1024]{1,0:T(8,128)(2,1)S(1)}, bf16[2048,1024]{1,0:T(8,128)(2,1)S(1)}, bf16[8,16,4096]{2,1,0:T(8,128)(2,1)S(1)}, bf16[8,16,4096]{2,1,0:T(8,128)(2,1)S(1)}, f32[8,128]{1,0:T(8,128)S(1)}) custom-call(s32[256]{0:T(256)} %slot_ref.1, s32[12,128]{1,0:T(8,128)} %bitcast.3, bf16[2048,1024]{1,0:T(8,128)(2,1)} %q_hbm.1, ...), custom_call_target="tpu_custom_call" | custom-call | tf_op jit(solution)/shard_map/attention/pallas_call | solution.py:488
  124.9 4.0 %deliver.1 = (bf16[2048,1024]{1,0:T(8,128)(2,1)}, bf16[2048,1024]{1,0:T(8,128)(2,1)}, bf16[8,16,4096]{2,1,0:T(8,128)(2,1)}, bf16[8,16,4096]{2,1,0:T(8,128)(2,1)}, f32[8,128]{1,0:T(8,128)}) custom-call(bf16[2048,1024]{1,0:T(8,128)(2,1)S(1)} %get-tuple-element.15.refs_0_, bf16[2048,1024]{1,0:T(8,128)(2,1)S(1)} %get-tuple-element.16.refs_1_, ...), custom_call_target="tpu_custom_call" | custom-call | tf_op jit(solution)/shard_map/deliver/pallas_call | solution.py:472

commit v4 on v3

--- a/solution.py
+++ b/solution.py
@@ -148,18 +148,17 @@
         for one in copies:
             one.start()
 
-    barrier = pltpu.get_barrier_semaphore()
-
-    @pl.loop(1, NEAR)
-    def _(j):
-        pl.semaphore_signal(barrier, inc=1, device_id=at_near(j // 8, j % 8), device_id_type=MESH)
-
-    for k in range(1, 4):
-        pl.semaphore_signal(barrier, inc=1, device_id=at_x(k), device_id_type=MESH)
-
     staged = [
         pltpu.make_async_copy(src, dst, lr.at[i]) for i, (src, dst) in enumerate(((lk_hbm, lk), (lv_hbm, lv)))]
     start(staged)
+
+    barrier = pltpu.get_barrier_semaphore()
+
+    for j in range(1, NEAR):
+        pl.semaphore_signal(barrier, inc=1, device_id=at_near(j // 8, j % 8), device_id_type=MESH)
+
+    for k in range(1, 4):
+        pl.semaphore_signal(barrier, inc=1, device_id=at_x(k), device_id_type=MESH)
 
     @pl.loop(0, HEADS)
     def _(h):

time: 129 us -> 129 us (level)
  no operation moved by 1% of the time
where the time goes in v4:
time: 129 us
  Pallas kernels  128 us (99%)
    pallas_call x1, Pallas kernels, local(): pl.pallas_call(kernel, out_shape=[pltpu.VMEM(queries.shape, bf16), pltpu....  124 us
    pallas_call x1, Pallas kernels, delivered(): pl.pallas_call(deliver, in_specs=[anywhere] * len(arrays), out_specs=[any...  3.98 us

profile of v4, /device:TPU:1, one launch (start us, length us, event | category | flops | bytes accessed | tf_op | source)
XLA Modules:
  0.0 128.7 jit_solution(7419637677212817985)
XLA Ops:
  0.6 124.0 %attention.1 = (bf16[2048,1024]{1,0:T(8,128)(2,1)S(1)}, bf16[2048,1024]{1,0:T(8,128)(2,1)S(1)}, bf16[8,16,4096]{2,1,0:T(8,128)(2,1)S(1)}, bf16[8,16,4096]{2,1,0:T(8,128)(2,1)S(1)}, f32[8,128]{1,0:T(8,128)S(1)}) custom-call(s32[256]{0:T(256)} %slot_ref.1, s32[12,128]{1,0:T(8,128)} %bitcast.3, bf16[2048,1024]{1,0:T(8,128)(2,1)} %q_hbm.1, ...), custom_call_target="tpu_custom_call" | custom-call | tf_op jit(solution)/shard_map/attention/pallas_call | solution.py:487
  124.7 4.0 %deliver.1 = (bf16[2048,1024]{1,0:T(8,128)(2,1)}, bf16[2048,1024]{1,0:T(8,128)(2,1)}, bf16[8,16,4096]{2,1,0:T(8,128)(2,1)}, bf16[8,16,4096]{2,1,0:T(8,128)(2,1)}, f32[8,128]{1,0:T(8,128)}) custom-call(bf16[2048,1024]{1,0:T(8,128)(2,1)S(1)} %get-tuple-element.15.refs_0_, bf16[2048,1024]{1,0:T(8,128)(2,1)S(1)} %get-tuple-element.16.refs_1_, ...), custom_call_target="tpu_custom_call" | custom-call | tf_op jit(solution)/shard_map/deliver/pallas_call | solution.py:471
